TPU v7x, 256 devices: a whole 4x4x8 slice. The times are simulated.
256 devices in a mesh: group: 32 (over y, x, core), tensor: 8 (over z).
Axes of the slice: x: 4, y: 4, z: 8, core: 2. Of those that a mesh axis runs over, the one named last changes fastest.
Arguments:
- owner: int32 [1024, 1], P('group'), may hold values from 0 to 31; in each aligned block of 32 rows (0 to 31, 32 to 63, ...) at most 2 rows name the same one
- cont_q: bfloat16 [1024, 8, 8192], P('group', None, 'tensor'), may hold values from -360 to 360
- continuation_keys: bfloat16 [1024, 8, 1024], P('group', None, 'tensor'), may hold values from -6 to 6
- continuation_values: bfloat16 [1024, 8, 1024], P('group', None, 'tensor'), may hold values from -6 to 6
- cached_prompt_keys: bfloat16 [32, 4096, 1024], P('group', None, 'tensor'), may hold values from -6 to 6
- cached_prompt_values: bfloat16 [32, 4096, 1024], P('group', None, 'tensor'), may hold values from -6 to 6
- out_weight: bfloat16 [8192, 8192], P('tensor', 'group'), may hold values from -0.0625 to 0.0625
Outputs:
- projected: bfloat16 [8192, 8192], P('group', 'tensor')
Inputs may be any that keep to these rules, and one draw needn't show every extreme that they name: `owner`: among the 32 continuations of each group (rows g * 32 to (g + 1) * 32 - 1) no prompt is named more than 2 times, a bound that some block reaches. Every prompt has a continuation somewhere; a continuation may sit on its own prompt's group.
All inputs are finite; a program needn't handle non-finite values.
Results may differ from a plain program's by a relative error of at most 0.0057.
Values may be sent and summed in bfloat16 or wider, within the bound.
No kernel may reach another device: no remote copies, remote signals or barrier semaphores. Data moves between devices by JAX's collectives and lax.ppermute only.
A program may use at most 128 MiB of HBM per device.

v0:
```python
import math

import jax
import jax.numpy as jnp
from jax import lax
from jax.sharding import PartitionSpec as P

HEAD_DIMENSION = 128


def prefix_partial(query, keys, values):
    count, steps, width = query.shape
    heads = keys.shape[1] // HEAD_DIMENSION
    block = math.gcd(count, 8)
    key_heads = keys.reshape(keys.shape[0], heads, HEAD_DIMENSION)
    value_heads = values.reshape(values.shape[0], heads, HEAD_DIMENSION)

    def one_block(rows):
        split = rows.reshape(block, steps, heads, -1, HEAD_DIMENSION)
        scores = jnp.einsum(
            "bcjgd,ljd->bcjgl", split, key_heads, preferred_element_type=jnp.float32
        ) * HEAD_DIMENSION ** (-0.5)
        top = jnp.max(scores, axis=-1)
        expd = jnp.exp(scores - top[..., None])
        total = jnp.sum(expd, axis=-1)
        summed = jnp.einsum(
            "bcjgl,ljd->bcjgd",
            expd.astype(jnp.bfloat16),
            value_heads,
            preferred_element_type=jnp.float32,
        )
        return (summed / total[..., None], top, total)

    outs, tops, totals = lax.map(one_block, query.reshape(count // block, block, steps, width))
    return (
        outs.reshape(count, steps, -1, HEAD_DIMENSION),
        tops.reshape(count, steps, -1),
        totals.reshape(count, steps, -1),
    )


def own_partial(query, keys, values):
    count, steps, width = query.shape
    heads = keys.shape[2] // HEAD_DIMENSION
    split = query.reshape(count, steps, heads, -1, HEAD_DIMENSION)
    key_heads = keys.reshape(count, steps, heads, HEAD_DIMENSION)
    value_heads = values.reshape(count, steps, heads, HEAD_DIMENSION)
    scores = jnp.einsum(
        "bcjgd,bejd->bcjge", split, key_heads, preferred_element_type=jnp.float32
    ) * HEAD_DIMENSION ** (-0.5)
    allowed = jnp.arange(steps)[None, :] <= jnp.arange(steps)[:, None]
    scores = jnp.where(allowed[None, :, None, None, :], scores, -1e30)
    top = jnp.max(scores, axis=-1)
    expd = jnp.exp(scores - top[..., None])
    total = jnp.sum(expd, axis=-1)
    summed = jnp.einsum(
        "bcjge,bejd->bcjgd",
        expd.astype(jnp.bfloat16),
        value_heads,
        preferred_element_type=jnp.float32,
    )
    return (
        (summed / total[..., None]).reshape(count, steps, -1, HEAD_DIMENSION),
        top.reshape(count, steps, -1),
        total.reshape(count, steps, -1),
    )


def combine(first, second):
    out_a, top_a, tot_a = first
    out_b, top_b, tot_b = second
    peak = jnp.maximum(top_a, top_b)
    weight_a = jnp.exp(top_a - peak) * tot_a
    weight_b = jnp.exp(top_b - peak) * tot_b
    mixed = (weight_a[..., None] * out_a + weight_b[..., None] * out_b) / (weight_a + weight_b)[
        ..., None
    ]
    return mixed.reshape(mixed.shape[0], mixed.shape[1], -1).astype(jnp.bfloat16)


def shards(
    owner,
    cont_q,
    continuation_keys,
    continuation_values,
    cached_prompt_keys,
    cached_prompt_values,
    out_weight,
):
    groups = lax.axis_size("group")
    host = cont_q.shape[0]
    steps = cont_q.shape[1]
    slot = max(2, 2 * host // groups)
    target = owner[:, 0]
    onehot = (target[:, None] == jnp.arange(groups, dtype=jnp.int32)[None, :]).astype(jnp.int32)
    rank = jnp.sum(jnp.cumsum(onehot, axis=0) * onehot, axis=1) - 1
    position = target * slot + rank
    prompt_keys = cached_prompt_keys[0]
    prompt_values = cached_prompt_values[0]

    def unpack(values):
        return jnp.take(values.reshape((groups * slot,) + values.shape[2:]), position, axis=0)

    buffer = jnp.zeros((groups * slot,) + cont_q.shape[1:], cont_q.dtype).at[position].set(cont_q)
    received = lax.all_to_all(
        buffer.reshape((groups, slot) + cont_q.shape[1:]),
        "group",
        split_axis=0,
        concat_axis=0,
        tiled=True,
    )
    sources = received.shape[0]
    items = received.shape[1]
    outs, tops, totals = prefix_partial(
        received.reshape((sources * items,) + received.shape[2:]), prompt_keys, prompt_values
    )
    outs = outs.reshape(sources, items, steps, -1)
    tops = tops.reshape(sources, items, steps, -1)
    totals = totals.reshape(sources, items, steps, -1)
    outs, tops, totals = (
        lax.all_to_all(outs, "group", split_axis=0, concat_axis=0, tiled=True),
        lax.all_to_all(tops, "group", split_axis=0, concat_axis=0, tiled=True),
        lax.all_to_all(totals, "group", split_axis=0, concat_axis=0, tiled=True),
    )
    first = (unpack(outs).reshape(host, steps, -1, HEAD_DIMENSION), unpack(tops), unpack(totals))
    second = own_partial(cont_q, continuation_keys, continuation_values)
    attn = combine(first, second)
    flat = attn.reshape(host * steps, -1)
    partial_out = jnp.dot(
        flat,
        lax.all_gather(out_weight, "group", axis=1, tiled=True),
        preferred_element_type=jnp.float32,
    )
    return lax.psum_scatter(partial_out, "tensor", scatter_dimension=1, tiled=True).astype(
        jnp.bfloat16
    )


def solution(mesh):
    in_specs = (
        P("group", None),
        P("group", None, "tensor"),
        P("group", None, "tensor"),
        P("group", None, "tensor"),
        P("group", None, "tensor"),
        P("group", None, "tensor"),
        P("tensor", "group"),
    )
    out_specs = P("group", "tensor")
    return jax.shard_map(shards, mesh=mesh, in_specs=in_specs, out_specs=out_specs, check_vma=False)
```

profile of v0, /device:TPU:1, one launch (start us, length us, event | category | flops | bytes accessed | tf_op | source)
XLA Modules:
  0.0 273.3 jit_solution(11469952571290943573)
XLA Ops:
  9.4 1.2 and_bitcast_fusion
  10.6 1.1 broadcast_in_dim.65
  11.7 4.8 %scatter_fusion = bf16[64,8,1024]{2,1,0:T(8,128)(2,1)} fusion(bf16[64,8,1024]{2,1,0:T(8,128)(2,1)} %broadcast_in_dim.65, s32[32]{0:T(128)S(1)} %bitcast.197, bf16[32,8,1024]{2,1,0:T(8,128)(2,1)} %param.12), kind=kCustom, calls=%fused_computation.3 | custom fusion | bytes 1572992 | tf_op jit(solution)/shard_map/scatter | solution.py:104
  16.5 8.6 %all-to-all-start = ((bf16[32,2,8,1024]{3,2,1,0:T(8,128)(2,1)}), bf16[32,2,8,1024]{3,2,1,0:T(8,128)(2,1)S(1)}, u32[]{:S(2)}, u32[]{:S(2)}) async-start(bf16[32,2,8,1024]{3,2,1,0:T(8,128)(2,1)} %bitcast.21), calls=%async_computation | async-start | bytes 2097152 | tf_op jit(solution)/shard_map/all_to_all | solution.py:105
  25.2 22.7 %all-to-all-done = bf16[32,2,8,1024]{3,2,1,0:T(8,128)(2,1)S(1)} async-done(((bf16[32,2,8,1024]{3,2,1,0:T(8,128)(2,1)}), bf16[32,2,8,1024]{3,2,1,0:T(8,128)(2,1)S(1)}, u32[]{:S(2)}, u32[]{:S(2)}) %all-to-all-start) | async-done | bytes 1048608 | tf_op jit(solution)/shard_map/all_to_all | solution.py:105
  47.8 50.1 %while.14 = (s32[]{:T(128)}, f32[8,8,8,1,8,128]{5,4,2,1,3,0:T(8,128)S(1)}, f32[8,8,8,1,8]{4,2,1,3,0:T(8,128)S(1)}, f32[8,8,8,1,8]{4,2,1,3,0:T(8,128)}, bf16[8,8,...) while((s32[]{:T(128)}, ...), condition=%wide.region_6.7_spmd, body=%wide.region_3.6_spmd.sunk | while | flops 1090583552 | bytes 32316024 | solution.py:34
  47.8 2.7 bitcast_reduce_fusion.2
  50.5 1.5 fusion.62
  52.6 1.4 fusion.63
  54.1 2.6 bitcast_reduce_fusion.2
  56.8 1.5 fusion.62
  58.9 1.4 fusion.63
  60.4 2.6 bitcast_reduce_fusion.2
  63.0 1.5 fusion.62
  65.2 1.4 fusion.63
  66.6 2.7 bitcast_reduce_fusion.2
  69.3 1.5 fusion.62
  71.5 1.4 fusion.63
  73.0 2.6 bitcast_reduce_fusion.2
  75.6 1.5 fusion.62
  77.7 1.4 fusion.63
  79.2 2.6 bitcast_reduce_fusion.2
  81.9 1.5 fusion.62
  84.0 1.4 fusion.63
  85.5 2.6 bitcast_reduce_fusion.2
  88.1 1.5 fusion.62
  90.3 1.4 fusion.63
  91.7 2.6 bitcast_reduce_fusion.2
  94.4 1.5 fusion.62
  96.5 1.4 fusion.63
  98.7 3.9 %all-to-all-start.1 = ((f32[32,1,128]{2,1,0:T(1,128)}), f32[32,1,128]{2,1,0:T(1,128)S(1)}, u32[]{:S(2)}, u32[]{:S(2)}) async-start(f32[32,1,128]{2,1,0:T(1,128)} %reshape.179), calls=%async_computation.1 | async-start | bytes 32768 | tf_op jit(solution)/shard_map/all_to_all | solution.py:122
  102.7 1.7 reshape.177
  104.4 5.2 %all-to-all-done.1 = f32[32,1,128]{2,1,0:T(1,128)S(1)} async-done(((f32[32,1,128]{2,1,0:T(1,128)}), f32[32,1,128]{2,1,0:T(1,128)S(1)}, u32[]{:S(2)}, u32[]{:S(2)}) %all-to-all-start.1) | async-done | bytes 16416 | tf_op jit(solution)/shard_map/all_to_all | solution.py:122
  109.6 4.1 %all-to-all-start.2 = ((f32[32,1,128]{2,1,0:T(1,128)}), f32[32,1,128]{2,1,0:T(1,128)S(1)}, u32[]{:S(2)}, u32[]{:S(2)}) async-start(f32[32,1,128]{2,1,0:T(1,128)} %reshape.177), calls=%async_computation.2 | async-start | bytes 32768 | tf_op jit(solution)/shard_map/all_to_all | solution.py:123
  113.7 1.5 reshape_reshape.15
  115.3 5.5 %all-to-all-done.2 = f32[32,1,128]{2,1,0:T(1,128)S(1)} async-done(((f32[32,1,128]{2,1,0:T(1,128)}), f32[32,1,128]{2,1,0:T(1,128)S(1)}, u32[]{:S(2)}, u32[]{:S(2)}) %all-to-all-start.2) | async-done | bytes 16416 | tf_op jit(solution)/shard_map/all_to_all | solution.py:123
  120.8 4.3 %all-to-all-start.3 = ((f32[32,2,8,1024]{3,2,1,0:T(8,128)}), f32[32,2,8,1024]{3,2,1,0:T(8,128)S(1)}, u32[]{:S(2)}, u32[]{:S(2)}) async-start(f32[32,2,8,1024]{3,2,1,0:T(8,128)} %reshape_reshape.15), calls=%async_computation.3 | async-start | bytes 4194304 | tf_op jit(solution)/shard_map/all_to_all | solution.py:121
  125.4 3.5 %fusion.54 = (f32[32,8,8]{2,1,0:T(8,128)S(1)}, f32[32,8,1,8,8]{3,4,1,0,2:T(8,128)S(1)}) fusion(bf16[32,8,8,128]{3,1,2,0:T(8,128)(2,1)} %bitcast.190, bf16[32,8,128]{2,1,0:T(8,128)(2,1)S(1)} %copy-done.2, pred[8,8]{1,0:T(8,128)(4,1)S(1)} %iota_compare_fusion.1), kind=kOutput, calls=%fused_computation.68 | convolution fusion | flops 4241408 | bytes 663616 | tf_op jit(solution)/shard_map/bcjgd,bejd->bcjge/dot_general | solution.py:48
  129.5 1.3 broadcast_in_dim.68
  130.7 1.4 broadcast_in_dim.69
  132.1 1.2 pad_clamp_fusion
  133.3 1.1 compare_and_fusion
  135.0 1.6 divide_bitcast_fusion
  138.7 1.4 reduce.5
  142.7 10.3 %all-to-all-done.3 = f32[32,2,8,1024]{3,2,1,0:T(8,128)S(1)} async-done(((f32[32,2,8,1024]{3,2,1,0:T(8,128)}), f32[32,2,8,1024]{3,2,1,0:T(8,128)S(1)}, u32[]{:S(2)}, u32[]{:S(2)}) %all-to-all-start.3) | async-done | bytes 2097184 | tf_op jit(solution)/shard_map/all_to_all | solution.py:121
  153.8 14.5 %fusion.34 = f32[256,8192]{1,0:T(8,128)} fusion(bf16[1024,8192]{1,0:T(8,128)(2,1)} %all-gather.2.cloned.1.call-done, f32[32,8,8,128]{3,2,1,0:T(8,128)} %divide_bitcast_fusion, f32[32,8,1024]{2,1,0:T(8,128)S(1)} %gather_fusion, f32[32,8,8]{1,2,0:T(8,128)} %copy.43, f32[32,8,8]{1,2,0:T(8,128)S(1)} %copy.41, f32[32,8,8]{1,2,0:T(8,128)S(1)} %copy.38, ...), kind=kOutput, calls=%fused_computation.39 | convolution fusion | flops 4296540160 | bytes 27287808 | tf_op jit(solution)/shard_map/dot_general | solution.py:129
  168.4 96.0 %reduce-scatter.2.cloned.1.call-done = f32[256,1024]{1,0:T(8,128)} async-done(((f32[256,8192]{1,0:T(8,128)}), f32[256,1024]{1,0:T(8,128)}) %reduce-scatter.2.cloned.1.call-update) | async-done | bytes 1048592 | tf_op jit(solution)/shard_map/reduce_scatter | solution.py:134
  264.4 2.1 convert_element_type.19
  (72 shorter events, 15.7 us)
Async XLA Ops:
  6.5 128.5 %copy-start = (bf16[32,8,128]{2,1,0:T(8,128)(2,1)S(1)}, bf16[32,8,128]{2,1,0:T(8,128)(2,1)}, u32[]{:S(2)}) copy-start(bf16[32,8,128]{2,1,0:T(8,128)(2,1)} %param.14) | copy-start | bytes 196612
  6.5 147.3 %all-gather.2.cloned.1.call-start = ((), (), s32[]{:S(2)}) async-start(), calls=%async_computation.5 | async-start | bytes 17301504 | tf_op jit(solution)/shard_map/all_gather | solution.py:131
  8.9 0.5 copy-start.5
  10.6 5.9 %copy-start.4 = (s32[32,1]{0,1:T(1,128)}, s32[32,1]{0,1:T(1,128)S(1)}, u32[]{:S(2)}) copy-start(s32[32,1]{0,1:T(1,128)S(1)} %get-tuple-element.63) | copy-start | bytes 388
  16.5 31.3 %all-to-all-start = ((bf16[32,2,8,1024]{3,2,1,0:T(8,128)(2,1)}), bf16[32,2,8,1024]{3,2,1,0:T(8,128)(2,1)S(1)}, u32[]{:S(2)}, u32[]{:S(2)}) async-start(bf16[32,2,8,1024]{3,2,1,0:T(8,128)(2,1)} %bitcast.21), calls=%async_computation | async-start | bytes 2097152 | tf_op jit(solution)/shard_map/all_to_all | solution.py:105
  47.8 4.8 %copy-start.1 = (bf16[4096,1,128]{2,0,1:T(8,128)(2,1)S(1)}, bf16[4096,1,128]{2,0,1:T(8,128)(2,1)}, u32[]{:S(2)}) copy-start(bf16[4096,1,128]{2,0,1:T(8,128)(2,1)} %get-tuple-element.148) | copy-start | bytes 3145732 | tf_op jit(solution)/shard_map/while
  54.1 4.8 %copy-start.1 = (bf16[4096,1,128]{2,0,1:T(8,128)(2,1)S(1)}, bf16[4096,1,128]{2,0,1:T(8,128)(2,1)}, u32[]{:S(2)}) copy-start(bf16[4096,1,128]{2,0,1:T(8,128)(2,1)} %get-tuple-element.148) | copy-start | bytes 3145732 | tf_op jit(solution)/shard_map/while
  60.4 4.8 %copy-start.1 = (bf16[4096,1,128]{2,0,1:T(8,128)(2,1)S(1)}, bf16[4096,1,128]{2,0,1:T(8,128)(2,1)}, u32[]{:S(2)}) copy-start(bf16[4096,1,128]{2,0,1:T(8,128)(2,1)} %get-tuple-element.148) | copy-start | bytes 3145732 | tf_op jit(solution)/shard_map/while
  66.6 4.8 %copy-start.1 = (bf16[4096,1,128]{2,0,1:T(8,128)(2,1)S(1)}, bf16[4096,1,128]{2,0,1:T(8,128)(2,1)}, u32[]{:S(2)}) copy-start(bf16[4096,1,128]{2,0,1:T(8,128)(2,1)} %get-tuple-element.148) | copy-start | bytes 3145732 | tf_op jit(solution)/shard_map/while
  72.9 4.8 %copy-start.1 = (bf16[4096,1,128]{2,0,1:T(8,128)(2,1)S(1)}, bf16[4096,1,128]{2,0,1:T(8,128)(2,1)}, u32[]{:S(2)}) copy-start(bf16[4096,1,128]{2,0,1:T(8,128)(2,1)} %get-tuple-element.148) | copy-start | bytes 3145732 | tf_op jit(solution)/shard_map/while
  79.2 4.8 %copy-start.1 = (bf16[4096,1,128]{2,0,1:T(8,128)(2,1)S(1)}, bf16[4096,1,128]{2,0,1:T(8,128)(2,1)}, u32[]{:S(2)}) copy-start(bf16[4096,1,128]{2,0,1:T(8,128)(2,1)} %get-tuple-element.148) | copy-start | bytes 3145732 | tf_op jit(solution)/shard_map/while
  85.5 4.8 %copy-start.1 = (bf16[4096,1,128]{2,0,1:T(8,128)(2,1)S(1)}, bf16[4096,1,128]{2,0,1:T(8,128)(2,1)}, u32[]{:S(2)}) copy-start(bf16[4096,1,128]{2,0,1:T(8,128)(2,1)} %get-tuple-element.148) | copy-start | bytes 3145732 | tf_op jit(solution)/shard_map/while
  91.7 4.8 %copy-start.1 = (bf16[4096,1,128]{2,0,1:T(8,128)(2,1)S(1)}, bf16[4096,1,128]{2,0,1:T(8,128)(2,1)}, u32[]{:S(2)}) copy-start(bf16[4096,1,128]{2,0,1:T(8,128)(2,1)} %get-tuple-element.148) | copy-start | bytes 3145732 | tf_op jit(solution)/shard_map/while
  98.0 27.4 %copy-start.2 = (bf16[32,8,128]{2,1,0:T(8,128)(2,1)S(1)}, bf16[32,8,128]{2,1,0:T(8,128)(2,1)}, u32[]{:S(2)}) copy-start(bf16[32,8,128]{2,1,0:T(8,128)(2,1)} %param.13) | copy-start | bytes 196612
  98.7 10.9 %all-to-all-start.1 = ((f32[32,1,128]{2,1,0:T(1,128)}), f32[32,1,128]{2,1,0:T(1,128)S(1)}, u32[]{:S(2)}, u32[]{:S(2)}) async-start(f32[32,1,128]{2,1,0:T(1,128)} %reshape.179), calls=%async_computation.1 | async-start | bytes 32768 | tf_op jit(solution)/shard_map/all_to_all | solution.py:122
  109.6 11.2 %all-to-all-start.2 = ((f32[32,1,128]{2,1,0:T(1,128)}), f32[32,1,128]{2,1,0:T(1,128)S(1)}, u32[]{:S(2)}, u32[]{:S(2)}) async-start(f32[32,1,128]{2,1,0:T(1,128)} %reshape.177), calls=%async_computation.2 | async-start | bytes 32768 | tf_op jit(solution)/shard_map/all_to_all | solution.py:123
  120.8 8.2 %copy-start.3 = (f32[32,1,128]{2,1,0:T(1,128)}, f32[32,1,128]{2,1,0:T(1,128)S(1)}, u32[]{:S(2)}) copy-start(f32[32,1,128]{2,1,0:T(1,128)S(1)} %all-to-all-done.2) | copy-start | bytes 49156
  120.8 32.3 %all-to-all-start.3 = ((f32[32,2,8,1024]{3,2,1,0:T(8,128)}), f32[32,2,8,1024]{3,2,1,0:T(8,128)S(1)}, u32[]{:S(2)}, u32[]{:S(2)}) async-start(f32[32,2,8,1024]{3,2,1,0:T(8,128)} %reshape_reshape.15), calls=%async_computation.3 | async-start | bytes 4194304 | tf_op jit(solution)/shard_map/all_to_all | solution.py:121
  125.1 139.3 %reduce-scatter.2.cloned.1.call-start = ((), (), s32[]{:S(2)}) async-start(), calls=%async_computation.6 | async-start | bytes 9437184 | tf_op jit(solution)/shard_map/reduce_scatter | solution.py:134
Sparse Core Ops, SparseCore 0:
  9.8 100.9 all-gather.1
  168.5 95.8 reduce-scatter.1
where the time goes:
time: 274 us; the launch traced here: 273 us
  waiting for transfers between devices  140 us (51%)
  matrix products  52.2 us (19%)
  other arithmetic  22.9 us (8%)
  local copies, waits for them, and re-layouts  22.6 us (8%)
  starting transfers between devices  21.2 us (8%)
  between operations  13.6 us (5%)
    reduce_scatter x1, waiting for transfers between devices, shards(): lax.psum_scatter(partial_out, 'tensor', scatter_dimension=1, tiled=True)  96 us
    all_to_all x1, waiting for transfers between devices, shards(): lax.all_to_all(buffer.reshape((groups, slot) + cont_q.shape[1:]), 'group'...  22.7 us
    dot_general x8, matrix products, one_block(): jnp.einsum('bcjgd,ljd->bcjgl', split, key_heads, preferred_element_type=j...  21.2 us
    dot_general x1, matrix products, shards(): jnp.dot(flat, lax.all_gather(out_weight, 'group', axis=1, tiled=True), pr...  14.5 us
    reduce_sum x8, other arithmetic, one_block(): total = jnp.sum(expd, axis=-1)  12 us
    dot_general x8, matrix products, one_block(): jnp.einsum('bcjgl,ljd->bcjgd', expd.astype(jnp.bfloat16), value_heads, pr...  11.4 us
    all_to_all x1, waiting for transfers between devices, shards(): lax.all_to_all(outs, 'group', split_axis=0, concat_axis=0, tiled=True)  10.3 us
    all_to_all x1, starting transfers between devices, shards(): lax.all_to_all(buffer.reshape((groups, slot) + cont_q.shape[1:]), 'group'...  8.6 us
  transfers between devices with their start and end apart: 6, of which 5 were waited for; matrix products, arithmetic and copies ran while one was open for 29% of the time, Pallas kernels for 0%

commit v1 on v0

v1 whole, which is shorter than its diff:
```python
import functools

import jax
import jax.numpy as jnp
from jax import lax
from jax.experimental import pallas as pl
from jax.experimental.pallas import tpu as pltpu
from jax.sharding import Mesh, PartitionSpec as P

HEAD = 128
GROUPS = 32
SLOT = 2
HOST = 32
STEPS = 8
HEADS = 8
PROMPT = 4096
RING = 8
GROUP = ("y", "x", "c")
PARTS = (4, 4)
SCALE2 = HEAD**-0.5 * 1.4426950408889634


def smem():
    return pl.BlockSpec(memory_space=pltpu.SMEM)


def vmem():
    return pl.BlockSpec(memory_space=pltpu.VMEM)


def hbm():
    return pl.BlockSpec(memory_space=pl.ANY)


def each_place(owner_ref, used_ref, act):
    for g in range(GROUPS):
        used_ref[g] = 0

    @pl.loop(0, HOST)
    def _(c):
        prompt = owner_ref[c, 0]
        rank = used_ref[prompt]
        used_ref[prompt] = rank + 1
        act(c, prompt * SLOT + rank)


def pack_kernel(owner_ref, q_ref, k_ref, v_ref, *rest):
    outs, used_ref = rest[:-1], rest[-1]
    for out in outs:
        out[...] = jnp.zeros_like(out)

    def act(c, place):
        first = 0
        for part, heads in enumerate(PARTS):
            width = heads * HEAD
            outs[part][place, :, 0:width] = q_ref[c, :, first : first + width]
            first += width
        width = PARTS[0] * HEAD
        outs[0][place, :, width : width + HEAD] = k_ref[c]
        outs[0][place, :, width + HEAD : width + 2 * HEAD] = v_ref[c]

    each_place(owner_ref, used_ref, act)


def pack(owner, q, k, v):
    widths = [heads * HEAD for heads in PARTS]
    widths[0] += 2 * HEAD
    return pl.pallas_call(
        pack_kernel,
        out_shape=[
            jax.ShapeDtypeStruct((GROUPS * SLOT, STEPS, width), jnp.bfloat16) for width in widths
        ],
        in_specs=[smem(), vmem(), vmem(), vmem()],
        out_specs=[vmem()] * len(PARTS),
        scratch_shapes=[pltpu.SMEM((GROUPS,), jnp.int32)],
        compiler_params=pltpu.CompilerParams(vmem_limit_bytes=16 * 2**20),
        name="pack",
    )(owner, q, k, v)


def unpack_kernel(owner_ref, got_ref, out_ref, used_ref):
    def act(c, place):
        out_ref[c] = got_ref[place]

    each_place(owner_ref, used_ref, act)


def unpack(owner, got):
    return pl.pallas_call(
        unpack_kernel,
        out_shape=jax.ShapeDtypeStruct((HOST,) + got.shape[1:], got.dtype),
        in_specs=[smem(), vmem()],
        out_specs=vmem(),
        scratch_shapes=[pltpu.SMEM((GROUPS,), jnp.int32)],
        compiler_params=pltpu.CompilerParams(vmem_limit_bytes=16 * 2**20),
        name="unpack",
    )(owner, got)


def prompt_kernel(k_ref, v_ref, after_ref, kt_ref, ve_ref):
    for first in range(0, PROMPT, 512):
        rows = slice(first, first + 512)
        kt_ref[:, rows] = k_ref[0, rows, :].astype(jnp.float32).T.astype(jnp.bfloat16)
        ve_ref[rows, 0:HEAD] = v_ref[0, rows, :]
        lane = lax.broadcasted_iota(jnp.int32, (512, HEAD), 1)
        ve_ref[rows, HEAD:] = jnp.where(lane == 0, 1.0, 0.0).astype(jnp.bfloat16)


def prompt_ready(keys, values, after):
    return pl.pallas_call(
        prompt_kernel,
        out_shape=[
            jax.ShapeDtypeStruct((HEAD, PROMPT), jnp.bfloat16),
            jax.ShapeDtypeStruct((PROMPT, 2 * HEAD), jnp.bfloat16),
        ],
        in_specs=[vmem(), vmem(), hbm()],
        out_specs=[vmem(), vmem()],
        compiler_params=pltpu.CompilerParams(vmem_limit_bytes=16 * 2**20),
        cost_estimate=pl.CostEstimate(flops=0, bytes_accessed=8 * 2**20, transcendentals=0),
        name="prompt_ready",
    )(keys, values, after)


TILE = 8
ROWS = 256


def attend_kernel(heads, start, tiles, block_cols, q_ref, own_ref, kt_ref, ve_ref, *refs):
    out_ref, scratch = refs[-7], refs[-6:]
    if start:
        out_ref[0 : start * TILE] = refs[0][...]
    each = TILE * STEPS
    base = PARTS[0] * HEAD
    s_refs, p_refs, peaks = scratch[0:2], scratch[2:4], scratch[4:6]

    def flat(ref, tile, first):
        block = ref[pl.ds((start + tile) * TILE, TILE), :, first : first + HEAD].astype(jnp.float32)
        return block.reshape(each, HEAD)

    def weights(scores, peak):
        return jnp.exp2((scores - peak) * SCALE2).astype(jnp.bfloat16)

    def stages(tile, slot, do):
        s_ref, peak_ref = s_refs[slot], peaks[slot]
        old_s, old_peak, new_p, old_p = s_refs[1 - slot], peaks[1 - slot], p_refs[1 - slot], p_refs[slot]
        top = None
        if do[0]:
            query = jnp.concatenate(
                [flat(q_ref, tile, h * HEAD) for h in range(heads)], axis=0
            ).astype(jnp.bfloat16)
            own_k = flat(own_ref, tile, base)
            own_k = jnp.concatenate([own_k, jnp.zeros_like(own_k)], axis=0).astype(jnp.bfloat16)
            own = lax.dot_general(
                query, own_k, (((1,), (1,)), ((), ())), preferred_element_type=jnp.float32
            )
            row = lax.rem(lax.broadcasted_iota(jnp.int32, own.shape, 0), each)
            col = lax.broadcasted_iota(jnp.int32, own.shape, 1)
            own = jnp.where((row // STEPS == col // STEPS) & (col <= row), own, -1e30)
            s_ref[:, PROMPT:] = own
            top = own
        if do[1]:
            peak = old_peak[...]
        if do[2]:
            own_v = flat(own_ref, tile - 2, base + HEAD)
            lane = lax.broadcasted_iota(jnp.int32, own_v.shape, 1)
            own_v = jnp.concatenate([own_v, jnp.where(lane == 0, 1.0, 0.0)], axis=1)
            own_v = jnp.concatenate([own_v, jnp.zeros_like(own_v)], axis=0).astype(jnp.bfloat16)
            acc = jnp.dot(old_p[:, PROMPT:], own_v, preferred_element_type=jnp.float32)
        for first in range(0, PROMPT, block_cols):
            part = slice(first, first + block_cols)
            if do[0]:
                scores = jnp.dot(query, kt_ref[:, part], preferred_element_type=jnp.float32)
                s_ref[:, part] = scores
                for lane in range(0, block_cols, HEAD):
                    top = jnp.maximum(top, scores[:, lane : lane + HEAD])
            if do[1]:
                for at in range(first, first + block_cols, HEAD):
                    new_p[:, at : at + HEAD] = weights(old_s[:, at : at + HEAD], peak)
            if do[2] and first % 1024 == 0:
                wide = slice(first, first + 1024)
                acc = acc + jnp.dot(
                    old_p[:, wide], ve_ref[wide, :], preferred_element_type=jnp.float32
                )
        if do[1]:
            new_p[:, PROMPT:] = weights(old_s[:, PROMPT:], peak)
        if do[0]:
            peak_ref[...] = jnp.broadcast_to(jnp.max(top, axis=1, keepdims=True), top.shape)
        if do[2]:
            out = acc[:, 0:HEAD] / acc[:, HEAD : HEAD + 1]
            for h in range(heads):
                out_ref[pl.ds((start + tile - 2) * TILE, TILE), :, h * HEAD : (h + 1) * HEAD] = (
                    out[h * each : (h + 1) * each].reshape(TILE, STEPS, HEAD).astype(jnp.bfloat16)
                )

    stages(0, 0, (True, False, False))
    stages(1, 1, (True, True, False))

    @pl.loop(1, tiles // 2)
    def _(pair):
        stages(2 * pair, 0, (True, True, True))
        stages(2 * pair + 1, 1, (True, True, True))

    stages(tiles, 0, (False, True, True))
    stages(tiles + 1, 1, (False, False, True))


def attend(heads, queries, own, keys, values, start, slots, before=(), cols=256):
    assert heads * TILE * STEPS == ROWS
    inputs = [queries, own, keys, values, *before]
    return pl.pallas_call(
        functools.partial(attend_kernel, heads, start // TILE, slots // TILE, cols),
        out_shape=jax.ShapeDtypeStruct((start + slots, STEPS, heads * HEAD), jnp.bfloat16),
        in_specs=[vmem()] * (4 + len(before)),
        out_specs=vmem(),
        scratch_shapes=[pltpu.VMEM((ROWS, PROMPT + HEAD), jnp.float32)] * 2
        + [pltpu.VMEM((ROWS, PROMPT + HEAD), jnp.bfloat16)] * 2
        + [pltpu.VMEM((ROWS, HEAD), jnp.float32)] * 2,
        compiler_params=pltpu.CompilerParams(vmem_limit_bytes=24 * 2**20),
        cost_estimate=pl.CostEstimate(
            flops=4 * slots * STEPS * heads * PROMPT * HEAD,
            bytes_accessed=4 * 2**20,
            transcendentals=slots * STEPS * heads * PROMPT,
        ),
        name="attend",
    )(*inputs)


def project_kernel(first, *refs):
    parts, refs = refs[: RING + 1], refs[RING + 1 :]
    before, refs = (refs[0], refs[1:]) if first else (None, refs)
    weight, out_ref, w_ref, acc_ref, sems = refs
    rows, width = parts[0].shape
    copies = {}
    order = (0, 1, 7, 2, 6, 3, 5, 4)
    for d in order:
        for r in range(4):
            copy = pltpu.make_async_copy(
                weight.at[(d - 4 * (r % 2)) % RING * 4 + r, pl.ds(first, width), :],
                w_ref.at[d, :, pl.ds(r * 256, 256)],
                sems.at[d, r],
            )
            copy.start()
            copies[d, r] = copy
    near = dict(zip((0, 1, 2, 3, 5, 6, 7), parts))
    for d in order:
        for r in range(4):
            copies[d, r].wait()
        if d == 4:
            left = jnp.concatenate([parts[RING - 1][...], parts[RING][...]], axis=0)
        else:
            left = near[d][...]
        for cols in (slice(0, 512), slice(512, 1024)):
            acc = jnp.dot(left, w_ref[d, :, cols], preferred_element_type=jnp.float32)
            if d != order[0]:
                acc = acc + acc_ref[:, cols]
            elif before is not None:
                acc = acc + before[:, cols]
            if d != order[-1]:
                acc_ref[:, cols] = acc
            else:
                out_ref[:, cols] = acc.astype(out_ref.dtype)


def project(parts, before, weight, first):
    rows, width = parts[0].shape
    last = first + width == HEADS * HEAD
    operands = list(parts) + ([before] if before is not None else [])
    return pl.pallas_call(
        functools.partial(project_kernel, first),
        out_shape=jax.ShapeDtypeStruct((rows, 1024), jnp.bfloat16 if last else jnp.float32),
        in_specs=[vmem()] * len(operands) + [hbm()],
        out_specs=vmem(),
        scratch_shapes=[
            pltpu.VMEM((RING, width, 1024), jnp.bfloat16),
            pltpu.VMEM((rows, 1024), jnp.float32),
            pltpu.SemaphoreType.DMA((RING, 4)),
        ],
        compiler_params=pltpu.CompilerParams(vmem_limit_bytes=50 * 2**20),
        cost_estimate=pl.CostEstimate(
            flops=2 * rows * 1024 * RING * width,
            bytes_accessed=RING * width * 1024 * 2 + rows * RING * width * 2,
            transcendentals=0,
        ),
        name="project",
    )(*operands, weight)


def hop(up, down):
    ahead = [(i, (i + 1) % RING) for i in range(RING)]
    back = [((i + 1) % RING, i) for i in range(RING)]
    return lax.ppermute(up, "z", ahead), lax.ppermute(down, "z", back)


def last_hop(up, down):
    half = up.shape[0] // 2
    return hop(up[:half], down[half:])


def exchange(block):
    shape = block.shape
    sent = block.reshape((GROUPS, SLOT) + shape[1:])
    got = lax.all_to_all(sent, GROUP, split_axis=0, concat_axis=0, tiled=True)
    return got.reshape(shape)


def weight_home():
    pairs = []
    for y in range(4):
        for x in range(4):
            for c in range(2):
                for z in range(RING):
                    to_z = y * 2 + x // 2
                    k = (z - to_z - 4 * c) % RING
                    to_y, to_x = k // 2, (k % 2) * 2 + x % 2
                    source = ((y * 4 + x) * 2 + c) * RING + z
                    pairs.append((source, ((to_y * 4 + to_x) * 2 + c) * RING + to_z))
    return pairs


def shards(owner, cont_q, own_keys, own_values, prompt_keys, prompt_values, out_weight):
    turned = lax.ppermute(out_weight, GROUP + ("z",), weight_home())
    packed = pack(owner, cont_q, own_keys, own_values)
    received = [exchange(block) for block in packed]
    turned, received[0] = lax.optimization_barrier((turned, received[0]))
    weight = lax.all_gather(turned, GROUP, axis=0)
    keys, values = prompt_ready(prompt_keys, prompt_values, packed[0])
    slots = GROUPS * SLOT
    rows = HOST * STEPS
    own = received[0]

    tie = lax.optimization_barrier
    attn = attend(PARTS[0], received[0], own, keys, values, 0, slots, cols=512)
    home = unpack(owner, exchange(attn)).reshape(rows, PARTS[0] * HEAD)
    query, home = tie((received[1], home))
    up_1, down_1 = hop(home, home)
    attn = attend(PARTS[1], query, own, keys, values, 0, slots // 2, cols=1024)
    attn, up_1, down_1 = tie((attn, up_1, down_1))
    up_2, down_2 = hop(up_1, down_1)
    attn = attend(PARTS[1], query, own, keys, values, slots // 2, slots // 2, (attn,), cols=1024)
    attn, up_2, down_2 = tie((attn, up_2, down_2))
    up_3, down_3 = hop(up_2, down_2)
    far = last_hop(up_3, down_3)
    first = (home, down_1, down_2, down_3, up_3, up_2, up_1) + far

    home = unpack(owner, exchange(attn)).reshape(rows, PARTS[1] * HEAD)
    up_1, down_1 = hop(home, home)
    up_2, down_2 = hop(up_1, down_1)
    up_3, down_3 = hop(up_2, down_2)
    far = last_hop(up_3, down_3)
    second = (home, down_1, down_2, down_3, up_3, up_2, up_1) + far
    result = project(first, None, weight, 0)
    return project(second, result, weight, PARTS[0] * HEAD)


def solution(mesh):
    mesh = Mesh(mesh.devices.reshape(4, 4, 2, 8), ("y", "x", "c", "z"))
    in_specs = (
        P(GROUP, None),
        P(GROUP, None, "z"),
        P(GROUP, None, "z"),
        P(GROUP, None, "z"),
        P(GROUP, None, "z"),
        P(GROUP, None, "z"),
        P("z", GROUP),
    )
    return jax.shard_map(
        shards, mesh=mesh, in_specs=in_specs, out_specs=P(GROUP, "z"), check_vma=False
    )
```

time: 274 us -> 227 us (0.83); the launches traced: 273 us -> 223 us
  waiting for transfers between devices: 140 us -> 74.9 us
  matrix products: 52.2 us -> 0 us
  Pallas kernels: 0 us -> 40 us
  blocking collectives: 0 us -> 37.8 us
  other arithmetic: 22.9 us -> 0 us
  starting transfers between devices: 21.2 us -> 43.5 us
  local copies, waits for them, and re-layouts: 22.6 us -> 13.5 us
    reduce_scatter x1 -> x0, waiting for transfers between devices: 96 us -> none  [shards(): lax.psum_scatter(partial_out, 'tensor', scatter_dimension=1, tiled=True)]
    dot_general x19 -> x0, matrix products: 52.2 us -> none  [the longest x8 21.2 us: one_block(): jnp.einsum('bcjgd,ljd->bcjgl', split, key_heads, preferred_element_type=j...]
    pallas_call x0 -> x9, Pallas kernels: none -> 40 us  [the longest x3 24.7 us: attend(): pl.pallas_call(functools.partial(attend_kernel, heads, start // TILE, slo...]
    all_to_all x0 -> x2, blocking collectives: none -> 37.8 us  [exchange(): got = lax.all_to_all(sent, GROUP, split_axis=0, concat_axis=0, tiled=True)]
    ppermute x0 -> x17, waiting for transfers between devices: none -> 34.5 us  [the longest x1 20.9 us: shards(): turned = lax.ppermute(out_weight, GROUP + ('z',), weight_home())]
    ppermute x0 -> x17, starting transfers between devices: none -> 30.1 us  [the longest x16 25.3 us: hop(): return (lax.ppermute(up, 'z', ahead), lax.ppermute(down, 'z', back))]
    reduce_sum x10 -> x0, other arithmetic: 13.3 us -> none  [the longest x8 12 us: one_block(): total = jnp.sum(expd, axis=-1)]
    unnamed x14 -> x33, local copies, waits for them, and re-layouts: 3.32 us -> 12.2 us
  transfers between devices with their start and end apart: 6 -> 20, of which waited for: 5 -> 8; matrix products, arithmetic and copies ran while one was open for 29% -> 1% of each run, Pallas kernels for 0% -> 14%
where the time goes in v1:
time: 227 us; the launch traced here: 223 us
  waiting for transfers between devices  74.9 us (33%)
  starting transfers between devices  43.5 us (19%)
  Pallas kernels  40 us (18%)
  blocking collectives  37.8 us (17%)
  between operations  13.6 us (6%)
  local copies, waits for them, and re-layouts  13.5 us (6%)
    all_to_all x2, waiting for transfers between devices, exchange(): got = lax.all_to_all(sent, GROUP, split_axis=0, concat_axis=0, tiled=True)  40.4 us
    all_to_all x2, blocking collectives, exchange(): got = lax.all_to_all(sent, GROUP, split_axis=0, concat_axis=0, tiled=True)  37.8 us
    ppermute x16, starting transfers between devices, hop(): return (lax.ppermute(up, 'z', ahead), lax.ppermute(down, 'z', back))  25.3 us
    pallas_call x3, Pallas kernels, attend(): pl.pallas_call(functools.partial(attend_kernel, heads, start // TILE, slo...  24.7 us
    ppermute x1, waiting for transfers between devices, shards(): turned = lax.ppermute(out_weight, GROUP + ('z',), weight_home())  20.9 us
    ppermute x16, waiting for transfers between devices, hop(): return (lax.ppermute(up, 'z', ahead), lax.ppermute(down, 'z', back))  13.6 us
    all_to_all x2, starting transfers between devices, exchange(): got = lax.all_to_all(sent, GROUP, split_axis=0, concat_axis=0, tiled=True)  13.4 us
    unnamed x33, local copies, waits for them, and re-layouts  12.2 us
  transfers between devices with their start and end apart: 20, of which 8 were waited for; matrix products, arithmetic and copies ran while one was open for 1% of the time, Pallas kernels for 14%

profile of v1, /device:TPU:1, one launch (start us, length us, event | category | flops | bytes accessed | tf_op | source)
XLA Modules:
  0.0 223.4 jit_solution(15643268336810553455)
XLA Ops:
  6.5 0.7 copy.10.owner_ref
  7.3 1.0 copy-done.2
  8.3 0.8 copy-done.9
  9.2 0.8 copy-done.10
  10.0 2.3 %pack.1 = (bf16[64,8,768]{2,1,0:T(8,128)(2,1)}, bf16[64,8,512]{2,1,0:T(8,128)(2,1)}) custom-call(s32[32,1]{1,0:T(8,128)S(1)} %copy.10.owner_ref, bf16[32,8,1024]{2,1,0:T(8,128)(2,1)S(1)} %copy-done.2, bf16[32,8,128]{2,1,0:T(8,128)(2,1)S(1)} %copy-done.9, bf16[32,8,128]{2,1,0:T(8,128)(2,1)S(1)} %copy-done.10), custom_call_target="tpu_custom_call" | custom-call | tf_op jit(solution)/shard_map/pack/pallas_call | solution.py:68
  12.3 8.6 %all-to-all-start.1 = ((bf16[32,2,8,768]{3,2,1,0:T(8,128)(2,1)}), bf16[32,2,8,768]{3,2,1,0:T(8,128)(2,1)S(1)}, u32[]{:S(2)}, u32[]{:S(2)}) async-start(bf16[32,2,8,768]{3,2,1,0:T(8,128)(2,1)} %bitcast.2), calls=%async_computation.1 | async-start | bytes 1572864 | tf_op jit(solution)/shard_map/all_to_all | solution.py:302
  21.0 4.8 %collective-permute-start = (bf16[1024,256]{1,0:T(8,128)(2,1)}, bf16[1024,256]{1,0:T(8,128)(2,1)S(1)}, u32[]{:S(2)}, u32[]{:S(2)}) collective-permute-start(bf16[1024,256]{1,0:T(8,128)(2,1)} %param.13), channel_id=1, source_target_pairs={{0,0},{1,32},{2,64},{3,96},{4,128},{5,160},{6,192},{7,224},{8,136}... | collective-permute-start | bytes 1572872 | tf_op jit(solution)/shard_map/ppermute | solution.py:321
  25.8 20.9 %collective-permute-done = bf16[1024,256]{1,0:T(8,128)(2,1)S(1)} collective-permute-done((bf16[1024,256]{1,0:T(8,128)(2,1)}, bf16[1024,256]{1,0:T(8,128)(2,1)S(1)}, u32[]{:S(2)}, u32[]{:S(2)}) %collective-permute-start) | collective-permute-done | bytes 524320 | tf_op jit(solution)/shard_map/ppermute | solution.py:321
  46.7 29.4 %all-to-all-done.1 = bf16[32,2,8,768]{3,2,1,0:T(8,128)(2,1)S(1)} async-done(((bf16[32,2,8,768]{3,2,1,0:T(8,128)(2,1)}), bf16[32,2,8,768]{3,2,1,0:T(8,128)(2,1)S(1)}, u32[]{:S(2)}, u32[]{:S(2)}) %all-to-all-start.1) | async-done | bytes 786464 | tf_op jit(solution)/shard_map/all_to_all | solution.py:302
  76.2 1.2 copy-done
  77.4 1.2 copy-done.1
  78.6 0.6 prompt_ready.1
  79.2 13.6 %attend.3 = bf16[64,8,512]{2,1,0:T(8,128)(2,1)S(1)} custom-call(bf16[64,8,768]{2,1,0:T(8,128)(2,1)S(1)} %bitcast.19, bf16[64,8,768]{2,1,0:T(8,128)(2,1)S(1)} %bitcast.20, bf16[128,4096]{1,0:T(8,128)(2,1)S(1)} %get-tuple-element.22.kt_ref, bf16[4096,256]{1,0:T(8,128)(2,1)S(1)} %get-tuple-element.23.ve_ref), custom_call_target="tpu_custom_call" | custom-call | flops 4294967296 | bytes 4194304 | tf_op jit(solution)/shard_map/attend/pallas_call | solution.py:210
  92.8 20.9 %all_to_all.20 = bf16[32,2,8,512]{3,2,1,0:T(8,128)(2,1)S(1)} all-to-all(bf16[32,2,8,512]{3,2,1,0:T(8,128)(2,1)S(1)} %bitcast.26), channel_id=1, replica_groups=mesh['y'=4,'x'=4,'c'=2,'z'=8] {'y','x','c'}, dimensions={0} | all-to-all | bytes 1048576 | tf_op jit(solution)/shard_map/all_to_all | solution.py:302
  113.7 4.8 %all-to-all-start = ((bf16[32,2,8,512]{3,2,1,0:T(8,128)(2,1)}), bf16[32,2,8,512]{3,2,1,0:T(8,128)(2,1)S(1)}, u32[]{:S(2)}, u32[]{:S(2)}) async-start(bf16[32,2,8,512]{3,2,1,0:T(8,128)(2,1)} %bitcast), calls=%async_computation | async-start | bytes 1048576 | tf_op jit(solution)/shard_map/all_to_all | solution.py:302
  118.6 1.1 unpack.2
  119.7 10.9 %all-to-all-done = bf16[32,2,8,512]{3,2,1,0:T(8,128)(2,1)S(1)} async-done(((bf16[32,2,8,512]{3,2,1,0:T(8,128)(2,1)}), bf16[32,2,8,512]{3,2,1,0:T(8,128)(2,1)S(1)}, u32[]{:S(2)}, u32[]{:S(2)}) %all-to-all-start) | async-done | bytes 524320 | tf_op jit(solution)/shard_map/all_to_all | solution.py:302
  130.6 0.2 collective-permute-start.1
  130.8 4.5 %collective-permute-start.2 = (bf16[256,512]{1,0:T(8,128)(2,1)S(1)}, bf16[256,512]{1,0:T(8,128)(2,1)S(1)}, u32[]{:S(2)}, u32[]{:S(2)}) collective-permute-start(bf16[256,512]{1,0:T(8,128)(2,1)S(1)} %bitcast.14), channel_id=1, source_target_pairs={{1,0},{2,1},{3,2},{4,3},{5,4},{6,5},{7,6},{0,7},{9,8},{10,9},{11,1... | collective-permute-start | bytes 786440 | tf_op jit(solution)/shard_map/ppermute | solution.py:291
  135.3 1.9 copy-done.12
  137.1 1.2 copy-done.14
  138.4 5.6 %attend.4.refs_0_ = bf16[32,8,512]{2,1,0:T(8,128)(2,1)S(1)} custom-call(bf16[64,8,512]{2,1,0:T(8,128)(2,1)S(1)} %bitcast.23, bf16[64,8,768]{2,1,0:T(8,128)(2,1)S(1)} %bitcast.21, bf16[128,4096]{1,0:T(8,128)(2,1)S(1)} %copy-done.14, bf16[4096,256]{1,0:T(8,128)(2,1)S(1)} %copy-done.12), custom_call_target="tpu_custom_call" | custom-call | flops 2147483648 | bytes 4194304 | tf_op jit(solution)/shard_map/attend/pallas_call | solution.py:210
  144.0 1.0 collective-permute-start.3
  144.9 1.8 collective-permute-start.4
  146.7 5.6 %attend.5 = bf16[64,8,512]{2,1,0:T(8,128)(2,1)S(1)} custom-call(bf16[64,8,512]{2,1,0:T(8,128)(2,1)S(1)} %bitcast.24, bf16[64,8,768]{2,1,0:T(8,128)(2,1)S(1)} %bitcast.22, bf16[128,4096]{1,0:T(8,128)(2,1)S(1)} %copy-done.14, bf16[4096,256]{1,0:T(8,128)(2,1)S(1)} %copy-done.12, bf16[32,8,512]{2,1,0:T(8,128)(2,1)S(1)} %attend.4.refs_0_), custom_call_target="tpu_custom_call" | custom-call | flops 2147483648 | bytes 4194304 | tf_op jit(solution)/shard_map/attend/pallas_call | solution.py:210
  152.3 0.1 collective-permute-done.3.refs_5_
  152.4 16.9 %all_to_all.21 = bf16[32,2,8,512]{3,2,1,0:T(8,128)(2,1)S(1)} all-to-all(bf16[32,2,8,512]{3,2,1,0:T(8,128)(2,1)S(1)} %bitcast.25), channel_id=1, replica_groups=mesh['y'=4,'x'=4,'c'=2,'z'=8] {'y','x','c'}, dimensions={0} | all-to-all | bytes 1048576 | tf_op jit(solution)/shard_map/all_to_all | solution.py:302
  169.3 1.1 unpack.3
  170.5 1.8 collective-permute-start.8
  172.2 2.3 %collective-permute-start.5 = (bf16[256,512]{1,0:T(8,128)(2,1)S(1)}, bf16[256,512]{1,0:T(8,128)(2,1)S(1)}, u32[]{:S(2)}, u32[]{:S(2)}) collective-permute-start(bf16[256,512]{1,0:T(8,128)(2,1)S(1)} %bitcast.17), channel_id=1, source_target_pairs={{1,0},{2,1},{3,2},{4,3},{5,4},{6,5},{7,6},{0,7},{9,8},{10,9},{11,1... | collective-permute-start | bytes 786440 | tf_op jit(solution)/shard_map/ppermute | solution.py:291
  174.6 5.8 %collective-permute-done.8.refs_6_ = bf16[256,512]{1,0:T(8,128)(2,1)S(1)} collective-permute-done((bf16[256,512]{1,0:T(8,128)(2,1)S(1)}, bf16[256,512]{1,0:T(8,128)(2,1)S(1)}, u32[]{:S(2)}, u32[]{:S(2)}) %collective-permute-start.8) | collective-permute-done | bytes 262176 | tf_op jit(solution)/shard_map/ppermute | solution.py:291
  180.3 2.7 %collective-permute-start.6 = (bf16[256,512]{1,0:T(8,128)(2,1)S(1)}, bf16[256,512]{1,0:T(8,128)(2,1)S(1)}, u32[]{:S(2)}, u32[]{:S(2)}) collective-permute-start(bf16[256,512]{1,0:T(8,128)(2,1)S(1)} %collective-permute-done.5.refs_1_), channel_id=1, source_target_pairs={{1,0},{2,1},{3,2},{4,3},{5,4},{6,5},{7,6},{0,7},{9,8},{10,9},{11,1... | collective-permute-start | bytes 786440 | tf_op jit(solution)/shard_map/ppermute | solution.py:291
  183.0 2.7 %collective-permute-start.13 = (bf16[256,512]{1,0:T(8,128)(2,1)S(1)}, bf16[256,512]{1,0:T(8,128)(2,1)S(1)}, u32[]{:S(2)}, u32[]{:S(2)}) collective-permute-start(bf16[256,512]{1,0:T(8,128)(2,1)S(1)} %collective-permute-done.4.refs_2_), channel_id=1, source_target_pairs={{1,0},{2,1},{3,2},{4,3},{5,4},{6,5},{7,6},{0,7},{9,8},{10,9},{11,1... | collective-permute-start | bytes 786440 | tf_op jit(solution)/shard_map/ppermute | solution.py:291
  185.7 2.2 collective-permute-done.9.refs_5_
  187.9 2.7 %collective-permute-start.7 = (bf16[256,512]{1,0:T(8,128)(2,1)S(1)}, bf16[256,512]{1,0:T(8,128)(2,1)S(1)}, u32[]{:S(2)}, u32[]{:S(2)}) collective-permute-start(bf16[256,512]{1,0:T(8,128)(2,1)S(1)} %collective-permute-done.6.refs_2_), channel_id=1, source_target_pairs={{1,0},{2,1},{3,2},{4,3},{5,4},{6,5},{7,6},{0,7},{9,8},{10,9},{11,1... | collective-permute-start | bytes 786440 | tf_op jit(solution)/shard_map/ppermute | solution.py:291
  190.6 2.9 %collective-permute-done.14.refs_4_ = bf16[256,512]{1,0:T(8,128)(2,1)S(1)} collective-permute-done((bf16[256,512]{1,0:T(8,128)(2,1)S(1)}, bf16[256,512]{1,0:T(8,128)(2,1)S(1)}, u32[]{:S(2)}, u32[]{:S(2)}) %collective-permute-start.14) | collective-permute-done | bytes 262176 | tf_op jit(solution)/shard_map/ppermute | solution.py:291
  193.5 0.3 collective-permute-start.15
  193.9 2.7 %collective-permute-start.16 = (bf16[128,512]{1,0:T(8,128)(2,1)S(1)}, bf16[128,512]{1,0:T(8,128)(2,1)S(1)}, u32[]{:S(2)}, u32[]{:S(2)}) collective-permute-start(bf16[128,512]{1,0:T(8,128)(2,1)S(1)} %slice.19), channel_id=1, source_target_pairs={{1,0},{2,1},{3,2},{4,3},{5,4},{6,5},{7,6},{0,7},{9,8},{10,9},{11,1... | collective-permute-start | bytes 393224 | tf_op jit(solution)/shard_map/ppermute | solution.py:291
  196.6 2.5 %collective-permute-done.10.refs_4_ = bf16[256,512]{1,0:T(8,128)(2,1)S(1)} collective-permute-done((bf16[256,512]{1,0:T(8,128)(2,1)S(1)}, bf16[256,512]{1,0:T(8,128)(2,1)S(1)}, u32[]{:S(2)}, u32[]{:S(2)}) %collective-permute-start.10) | collective-permute-done | bytes 262176 | tf_op jit(solution)/shard_map/ppermute | solution.py:291
  199.1 0.7 slice.16
  199.8 0.7 slice.17
  200.5 2.7 %collective-permute-start.12 = (bf16[128,512]{1,0:T(8,128)(2,1)}, bf16[128,512]{1,0:T(8,128)(2,1)}, u32[]{:S(2)}, u32[]{:S(2)}) collective-permute-start(bf16[128,512]{1,0:T(8,128)(2,1)} %slice.17), channel_id=1, source_target_pairs={{1,0},{2,1},{3,2},{4,3},{5,4},{6,5},{7,6},{0,7},{9,8},{10,9},{11,1... | collective-permute-start | bytes 393224 | tf_op jit(solution)/shard_map/ppermute | solution.py:291
  203.1 0.6 copy-done.5
  203.8 0.7 copy-done.7
  204.5 0.9 copy-done.6
  205.4 0.9 copy-done.8
  206.3 4.2 %project.2.refs_9_ = f32[256,1024]{1,0:T(8,128)S(1)} custom-call(bf16[256,512]{1,0:T(8,128)(2,1)S(1)} %bitcast.15, bf16[256,512]{1,0:T(8,128)(2,1)S(1)} %collective-permute-done.2.refs_1_, bf16[256,512]{1,0:T(8,128)(2,1)S(1)} %collective-permute-done.4.refs_2_, bf16[256,512]{1,0:T(8,128)(2,1)S(1)} %collective-permute-done.13.refs_3_, ...), custom_call_target="tpu_custom_call" | custom-call | flops 2147483648 | bytes 10485760 | tf_op jit(solution)/shard_map/project/pallas_call | solution.py:268
  210.6 6.0 %project.3 = bf16[256,1024]{1,0:T(8,128)(2,1)} custom-call(bf16[256,512]{1,0:T(8,128)(2,1)S(1)} %bitcast.18, bf16[256,512]{1,0:T(8,128)(2,1)S(1)} %collective-permute-done.5.refs_1_, bf16[256,512]{1,0:T(8,128)(2,1)S(1)} %copy-done.4, bf16[256,512]{1,0:T(8,128)(2,1)S(1)} %collective-permute-done.7.refs_3_, ...), custom_call_target="tpu_custom_call" | custom-call | flops 2147483648 | bytes 10485760 | tf_op jit(solution)/shard_map/project/pallas_call | solution.py:268
  (41 shorter events, 0.2 us)
Async XLA Ops:
  7.3 1.0 copy-start.2
  8.3 0.8 copy-start.9
  9.2 0.8 copy-start.10
  12.3 63.8 %all-to-all-start.1 = ((bf16[32,2,8,768]{3,2,1,0:T(8,128)(2,1)}), bf16[32,2,8,768]{3,2,1,0:T(8,128)(2,1)S(1)}, u32[]{:S(2)}, u32[]{:S(2)}) async-start(bf16[32,2,8,768]{3,2,1,0:T(8,128)(2,1)} %bitcast.2), calls=%async_computation.1 | async-start | bytes 1572864 | tf_op jit(solution)/shard_map/all_to_all | solution.py:302
  20.9 183.5 %all-gather.3.cloned.1.call-start = ((), (), s32[]{:S(2)}) async-start(), calls=%async_computation.4 | async-start | bytes 17301504 | tf_op jit(solution)/shard_map/all_gather | solution.py:325
  21.0 25.8 %collective-permute-start = (bf16[1024,256]{1,0:T(8,128)(2,1)}, bf16[1024,256]{1,0:T(8,128)(2,1)S(1)}, u32[]{:S(2)}, u32[]{:S(2)}) collective-permute-start(bf16[1024,256]{1,0:T(8,128)(2,1)} %param.13), channel_id=1, source_target_pairs={{0,0},{1,32},{2,64},{3,96},{4,128},{5,160},{6,192},{7,224},{8,136}... | collective-permute-start | bytes 1572872 | tf_op jit(solution)/shard_map/ppermute | solution.py:321
  46.7 29.4 %copy-start.15 = (bf16[1024,256]{1,0:T(8,128)(2,1)}, bf16[1024,256]{1,0:T(8,128)(2,1)S(1)}, u32[]{:S(2)}) copy-start(bf16[1024,256]{1,0:T(8,128)(2,1)S(1)} %collective-permute-done) | copy-start | bytes 1572868
  76.2 1.2 copy-start
  77.4 1.2 copy-start.1
  79.2 34.5 %copy-start.11 = (bf16[4096,256]{1,0:T(8,128)(2,1)}, bf16[4096,256]{1,0:T(8,128)(2,1)S(1)}, u32[]{:S(2)}) copy-start(bf16[4096,256]{1,0:T(8,128)(2,1)S(1)} %get-tuple-element.23.ve_ref) | copy-start | bytes 6291460
  79.2 34.5 %copy-start.13 = (bf16[128,4096]{1,0:T(8,128)(2,1)}, bf16[128,4096]{1,0:T(8,128)(2,1)S(1)}, u32[]{:S(2)}) copy-start(bf16[128,4096]{1,0:T(8,128)(2,1)S(1)} %get-tuple-element.22.kt_ref) | copy-start | bytes 3145732
  113.7 16.9 %all-to-all-start = ((bf16[32,2,8,512]{3,2,1,0:T(8,128)(2,1)}), bf16[32,2,8,512]{3,2,1,0:T(8,128)(2,1)S(1)}, u32[]{:S(2)}, u32[]{:S(2)}) async-start(bf16[32,2,8,512]{3,2,1,0:T(8,128)(2,1)} %bitcast), calls=%async_computation | async-start | bytes 1048576 | tf_op jit(solution)/shard_map/all_to_all | solution.py:302
  130.6 13.3 %collective-permute-start.1 = (bf16[256,512]{1,0:T(8,128)(2,1)S(1)}, bf16[256,512]{1,0:T(8,128)(2,1)S(1)}, u32[]{:S(2)}, u32[]{:S(2)}) collective-permute-start(bf16[256,512]{1,0:T(8,128)(2,1)S(1)} %bitcast.13), channel_id=1, source_target_pairs={{0,1},{1,2},{2,3},{3,4},{4,5},{5,6},{6,7},{7,0},{8,9},{9,10},{10,1... | collective-permute-start | bytes 786440 | tf_op jit(solution)/shard_map/ppermute | solution.py:291
  130.8 13.2 %collective-permute-start.2 = (bf16[256,512]{1,0:T(8,128)(2,1)S(1)}, bf16[256,512]{1,0:T(8,128)(2,1)S(1)}, u32[]{:S(2)}, u32[]{:S(2)}) collective-permute-start(bf16[256,512]{1,0:T(8,128)(2,1)S(1)} %bitcast.14), channel_id=1, source_target_pairs={{1,0},{2,1},{3,2},{4,3},{5,4},{6,5},{7,6},{0,7},{9,8},{10,9},{11,1... | collective-permute-start | bytes 786440 | tf_op jit(solution)/shard_map/ppermute | solution.py:291
  135.3 1.9 copy-start.12
  137.1 1.2 copy-start.14
  144.0 8.4 %collective-permute-start.3 = (bf16[256,512]{1,0:T(8,128)(2,1)S(1)}, bf16[256,512]{1,0:T(8,128)(2,1)S(1)}, u32[]{:S(2)}, u32[]{:S(2)}) collective-permute-start(bf16[256,512]{1,0:T(8,128)(2,1)S(1)} %collective-permute-done.1.refs_6_), channel_id=1, source_target_pairs={{0,1},{1,2},{2,3},{3,4},{4,5},{5,6},{6,7},{7,0},{8,9},{9,10},{10,1... | collective-permute-start | bytes 786440 | tf_op jit(solution)/shard_map/ppermute | solution.py:291
  144.9 7.5 %collective-permute-start.4 = (bf16[256,512]{1,0:T(8,128)(2,1)S(1)}, bf16[256,512]{1,0:T(8,128)(2,1)S(1)}, u32[]{:S(2)}, u32[]{:S(2)}) collective-permute-start(bf16[256,512]{1,0:T(8,128)(2,1)S(1)} %collective-permute-done.2.refs_1_), channel_id=1, source_target_pairs={{1,0},{2,1},{3,2},{4,3},{5,4},{6,5},{7,6},{0,7},{9,8},{10,9},{11,1... | collective-permute-start | bytes 786440 | tf_op jit(solution)/shard_map/ppermute | solution.py:291
  170.5 9.8 %collective-permute-start.8 = (bf16[256,512]{1,0:T(8,128)(2,1)S(1)}, bf16[256,512]{1,0:T(8,128)(2,1)S(1)}, u32[]{:S(2)}, u32[]{:S(2)}) collective-permute-start(bf16[256,512]{1,0:T(8,128)(2,1)S(1)} %bitcast.16), channel_id=1, source_target_pairs={{0,1},{1,2},{2,3},{3,4},{4,5},{5,6},{6,7},{7,0},{8,9},{9,10},{10,1... | collective-permute-start | bytes 786440 | tf_op jit(solution)/shard_map/ppermute | solution.py:291
  172.2 8.1 %collective-permute-start.5 = (bf16[256,512]{1,0:T(8,128)(2,1)S(1)}, bf16[256,512]{1,0:T(8,128)(2,1)S(1)}, u32[]{:S(2)}, u32[]{:S(2)}) collective-permute-start(bf16[256,512]{1,0:T(8,128)(2,1)S(1)} %bitcast.17), channel_id=1, source_target_pairs={{1,0},{2,1},{3,2},{4,3},{5,4},{6,5},{7,6},{0,7},{9,8},{10,9},{11,1... | collective-permute-start | bytes 786440 | tf_op jit(solution)/shard_map/ppermute | solution.py:291
  180.3 7.6 %collective-permute-start.9 = (bf16[256,512]{1,0:T(8,128)(2,1)S(1)}, bf16[256,512]{1,0:T(8,128)(2,1)S(1)}, u32[]{:S(2)}, u32[]{:S(2)}) collective-permute-start(bf16[256,512]{1,0:T(8,128)(2,1)S(1)} %collective-permute-done.8.refs_6_), channel_id=1, source_target_pairs={{0,1},{1,2},{2,3},{3,4},{4,5},{5,6},{6,7},{7,0},{8,9},{9,10},{10,1... | collective-permute-start | bytes 786440 | tf_op jit(solution)/shard_map/ppermute | solution.py:291
  180.3 7.6 %collective-permute-start.6 = (bf16[256,512]{1,0:T(8,128)(2,1)S(1)}, bf16[256,512]{1,0:T(8,128)(2,1)S(1)}, u32[]{:S(2)}, u32[]{:S(2)}) collective-permute-start(bf16[256,512]{1,0:T(8,128)(2,1)S(1)} %collective-permute-done.5.refs_1_), channel_id=1, source_target_pairs={{1,0},{2,1},{3,2},{4,3},{5,4},{6,5},{7,6},{0,7},{9,8},{10,9},{11,1... | collective-permute-start | bytes 786440 | tf_op jit(solution)/shard_map/ppermute | solution.py:291
  183.0 10.5 %collective-permute-start.14 = (bf16[256,512]{1,0:T(8,128)(2,1)S(1)}, bf16[256,512]{1,0:T(8,128)(2,1)S(1)}, u32[]{:S(2)}, u32[]{:S(2)}) collective-permute-start(bf16[256,512]{1,0:T(8,128)(2,1)S(1)} %collective-permute-done.3.refs_5_), channel_id=1, source_target_pairs={{0,1},{1,2},{2,3},{3,4},{4,5},{5,6},{6,7},{7,0},{8,9},{9,10},{10,1... | collective-permute-start | bytes 786440 | tf_op jit(solution)/shard_map/ppermute | solution.py:291
  183.0 10.9 %collective-permute-start.13 = (bf16[256,512]{1,0:T(8,128)(2,1)S(1)}, bf16[256,512]{1,0:T(8,128)(2,1)S(1)}, u32[]{:S(2)}, u32[]{:S(2)}) collective-permute-start(bf16[256,512]{1,0:T(8,128)(2,1)S(1)} %collective-permute-done.4.refs_2_), channel_id=1, source_target_pairs={{1,0},{2,1},{3,2},{4,3},{5,4},{6,5},{7,6},{0,7},{9,8},{10,9},{11,1... | collective-permute-start | bytes 786440 | tf_op jit(solution)/shard_map/ppermute | solution.py:291
  187.9 11.2 %collective-permute-start.10 = (bf16[256,512]{1,0:T(8,128)(2,1)S(1)}, bf16[256,512]{1,0:T(8,128)(2,1)S(1)}, u32[]{:S(2)}, u32[]{:S(2)}) collective-permute-start(bf16[256,512]{1,0:T(8,128)(2,1)S(1)} %collective-permute-done.9.refs_5_), channel_id=1, source_target_pairs={{0,1},{1,2},{2,3},{3,4},{4,5},{5,6},{6,7},{7,0},{8,9},{9,10},{10,1... | collective-permute-start | bytes 786440 | tf_op jit(solution)/shard_map/ppermute | solution.py:291
  187.9 11.9 %copy-start.3 = (bf16[256,512]{1,0:T(8,128)(2,1)}, bf16[256,512]{1,0:T(8,128)(2,1)S(1)}, u32[]{:S(2)}) copy-start(bf16[256,512]{1,0:T(8,128)(2,1)S(1)} %collective-permute-done.6.refs_2_) | copy-start | bytes 786436
  187.9 11.9 %collective-permute-start.7 = (bf16[256,512]{1,0:T(8,128)(2,1)S(1)}, bf16[256,512]{1,0:T(8,128)(2,1)S(1)}, u32[]{:S(2)}, u32[]{:S(2)}) collective-permute-start(bf16[256,512]{1,0:T(8,128)(2,1)S(1)} %collective-permute-done.6.refs_2_), channel_id=1, source_target_pairs={{1,0},{2,1},{3,2},{4,3},{5,4},{6,5},{7,6},{0,7},{9,8},{10,9},{11,1... | collective-permute-start | bytes 786440 | tf_op jit(solution)/shard_map/ppermute | solution.py:291
  193.5 9.6 %collective-permute-start.15 = (bf16[128,512]{1,0:T(8,128)(2,1)S(1)}, bf16[128,512]{1,0:T(8,128)(2,1)S(1)}, u32[]{:S(2)}, u32[]{:S(2)}) collective-permute-start(bf16[128,512]{1,0:T(8,128)(2,1)S(1)} %slice.18), channel_id=1, source_target_pairs={{0,1},{1,2},{2,3},{3,4},{4,5},{5,6},{6,7},{7,0},{8,9},{9,10},{10,1... | collective-permute-start | bytes 393224 | tf_op jit(solution)/shard_map/ppermute | solution.py:291
  193.9 9.9 %collective-permute-start.16 = (bf16[128,512]{1,0:T(8,128)(2,1)S(1)}, bf16[128,512]{1,0:T(8,128)(2,1)S(1)}, u32[]{:S(2)}, u32[]{:S(2)}) collective-permute-start(bf16[128,512]{1,0:T(8,128)(2,1)S(1)} %slice.19), channel_id=1, source_target_pairs={{1,0},{2,1},{3,2},{4,3},{5,4},{6,5},{7,6},{0,7},{9,8},{10,9},{11,1... | collective-permute-start | bytes 393224 | tf_op jit(solution)/shard_map/ppermute | solution.py:291
  199.8 10.7 %collective-permute-start.11 = (bf16[128,512]{1,0:T(8,128)(2,1)}, bf16[128,512]{1,0:T(8,128)(2,1)S(1)}, u32[]{:S(2)}, u32[]{:S(2)}) collective-permute-start(bf16[128,512]{1,0:T(8,128)(2,1)} %slice.16), channel_id=1, source_target_pairs={{0,1},{1,2},{2,3},{3,4},{4,5},{5,6},{6,7},{7,0},{8,9},{9,10},{10,1... | collective-permute-start | bytes 393224 | tf_op jit(solution)/shard_map/ppermute | solution.py:291
  200.5 10.1 %collective-permute-start.12 = (bf16[128,512]{1,0:T(8,128)(2,1)}, bf16[128,512]{1,0:T(8,128)(2,1)}, u32[]{:S(2)}, u32[]{:S(2)}) collective-permute-start(bf16[128,512]{1,0:T(8,128)(2,1)} %slice.17), channel_id=1, source_target_pairs={{1,0},{2,1},{3,2},{4,3},{5,4},{6,5},{7,6},{0,7},{9,8},{10,9},{11,1... | collective-permute-start | bytes 393224 | tf_op jit(solution)/shard_map/ppermute | solution.py:291
  203.1 0.6 copy-start.5
  203.8 0.7 copy-start.7
  204.5 6.1 %copy-start.4 = (bf16[256,512]{1,0:T(8,128)(2,1)S(1)}, bf16[256,512]{1,0:T(8,128)(2,1)}, u32[]{:S(2)}) copy-start(bf16[256,512]{1,0:T(8,128)(2,1)} %copy-done.3) | copy-start | bytes 786436
  204.5 0.9 copy-start.6
  205.4 0.9 copy-start.8
Sparse Core Ops, SparseCore 0:
  76.3 91.5 all-gather.2
